TPU v7x, 32 devices: a whole 2x2x4 slice. The times are simulated.
32 devices in a mesh: req: 16 (over z, x, core), tensor: 2 (over y).
Axes of the slice: x: 2, y: 2, z: 4, core: 2. Of those that a mesh axis runs over, the one named last changes fastest.
Arguments:
- tokens: bfloat16 [1024, 1024], P('req'), may hold values from -6 to 6
- norm_gain: float32 [1024], replicated, may hold values from 0.1 to 1.9
- w_qkv: bfloat16 [1024, 3, 1024], P(None, None, 'tensor'), may hold values from -0.1875 to 0.1875
- w_out: bfloat16 [1024, 1024], P('tensor'), may hold values from -0.25 to 0.25
- root_kv: bfloat16 [1024, 2, 1024], P('req', None, 'tensor'), may hold values from -60 to 60, as said below
- branch_kv: bfloat16 [16, 1024, 2, 1024], P('req', None, None, 'tensor'), may hold values from -60 to 60, as said below
- leaf_kv: bfloat16 [256, 16, 2, 1024], P('req', None, None, 'tensor'), may hold values from -60 to 60, as said below
- branch: int32 [256, 1], P('req'), may hold values from 0 to 15; in each aligned block of 16 rows (0 to 15, 16 to 31, ...) at most 2 rows name the same one
- node_owner: int32 [16], replicated, may hold values from 0 to 15, each once
- branch_len: int32 [16], replicated, may hold values from 1 to 1024, as said below
- leaf_len: int32 [256], P('req'), may hold values from 1 to 16
- new_count: int32 [256], P('req'), may hold values from 1 to 4
Outputs:
- attn_out: bfloat16 [1024, 1024], P('req', 'tensor')
Inputs may be any that keep to these rules, and one draw needn't show every extreme that they name: Among the 16 requests of one device (aligned blocks of rows) no branch node is named more than 2 times; some node is named exactly 2 times. `node_owner`: each storage slot holds exactly one node. `branch_len`: some node has all 1024 positions. `root_kv`: Real-valued keys and values. `branch_kv`: Real-valued keys and values. `leaf_kv`: Real-valued keys and values.
All inputs are finite; a program needn't handle non-finite values.
Results may differ from a plain program's by a relative error of at most 0.0095.
The roundings to bfloat16 on the way count: a program that leaves them out, or rounds other values in their place, can miss the bound.
Values may be sent and summed in bfloat16 or wider, within the bound.
A program may use at most 64 MiB of HBM per device.

v0:
```python
import jax
import jax.numpy as jnp
from jax import lax
from jax.sharding import PartitionSpec as P

HD = 64


floor_score = -1e30


def partial_softmax(queries, key_rows, value_rows, usable):
    scores = jnp.einsum(
        "qhe,khe->qhk", queries, key_rows, preferred_element_type=jnp.float32
    ) * HD ** (-0.5)
    masked = jnp.where(usable[:, None, :], scores, -jnp.inf)
    peak = jnp.max(masked, axis=2)
    weights = jnp.where(usable[:, None, :], jnp.exp(scores - peak[:, :, None]), 0.0)
    totals = jnp.sum(weights, axis=2)
    weighted = jnp.einsum(
        "qhk,khe->qhe", weights.astype(jnp.bfloat16), value_rows, preferred_element_type=jnp.float32
    )
    return (peak, totals, weighted)


def combine(first, second):
    peak = jnp.maximum(first[0], second[0])
    scale_one = jnp.exp(first[0] - peak)
    scale_two = jnp.exp(second[0] - peak)
    return (
        peak,
        first[1] * scale_one + second[1] * scale_two,
        first[2] * scale_one[..., None] + second[2] * scale_two[..., None],
    )


def empty_state(count, heads):
    return (
        jnp.full((count, heads), floor_score, jnp.float32),
        jnp.zeros((count, heads), jnp.float32),
        jnp.zeros((count, heads, HD), jnp.float32),
    )


def local(
    tokens,
    norm_gain,
    w_qkv,
    w_out,
    root_kv,
    branch_kv,
    leaf_kv,
    branch,
    node_owner,
    branch_len,
    leaf_len,
    new_count,
):
    rows = tokens.shape[0]
    requests = branch.shape[0]
    drafts = rows // requests
    nodes = node_owner.shape[0]
    width = w_out.shape[0]
    heads = width // HD
    capacity = max(2, 2 * requests // nodes)
    floats = tokens.astype(jnp.float32)
    normed = (
        floats * lax.rsqrt(jnp.mean(floats * floats, axis=1, keepdims=True) + 1e-05) * norm_gain
    ).astype(jnp.bfloat16)
    projected = jnp.dot(
        normed, w_qkv.reshape(w_qkv.shape[0], 3 * width), preferred_element_type=jnp.float32
    ).astype(jnp.bfloat16)
    queries = projected[:, :width]
    own_keys = projected[:, width : 2 * width]
    own_values = projected[:, 2 * width :]
    query_heads = queries.reshape(rows, heads, HD)
    piece = lax.all_gather(root_kv, "req", axis=0, tiled=True)
    usable = jnp.ones((rows, piece.shape[0]), jnp.bool_)
    found = partial_softmax(
        query_heads, piece[:, 0].reshape(-1, heads, HD), piece[:, 1].reshape(-1, heads, HD), usable
    )
    root_state = combine(empty_state(rows, heads), found)
    node_ids = jnp.arange(nodes, dtype=jnp.int32)
    chosen = branch == node_ids[None, :]
    target = jnp.sum(jnp.where(chosen, node_owner[None, :], 0), axis=1)
    order = jnp.arange(requests, dtype=jnp.int32)
    earlier = (target[:, None] == target[None, :]) & (order[None, :] < order[:, None])
    place = target * capacity + jnp.sum(earlier.astype(jnp.int32), axis=1)
    slot_ids = jnp.arange(nodes * capacity, dtype=jnp.int32)
    select = place[None, :] == slot_ids[:, None]
    outgoing = jnp.dot(
        select.astype(jnp.bfloat16),
        queries.reshape(requests, drafts * width),
        preferred_element_type=jnp.float32,
    )
    outgoing = outgoing.astype(jnp.bfloat16).reshape(nodes, capacity, drafts, width)
    owner_index = lax.axis_index("req")
    owned_length = jnp.sum(jnp.where(node_owner == owner_index, branch_len, 0))
    cache = branch_kv[0]
    span = cache.shape[0]
    incoming = lax.all_to_all(outgoing, "req", split_axis=0, concat_axis=0, tiled=True)
    items = incoming.shape[1]
    count = nodes * items * drafts
    asked = incoming.reshape(count, heads, HD)
    usable = jnp.broadcast_to(jnp.arange(span)[None, :] < owned_length, (count, span))
    state = partial_softmax(
        asked, cache[:, 0].reshape(span, heads, HD), cache[:, 1].reshape(span, heads, HD), usable
    )
    picker = select.astype(jnp.float32).T

    def pick_rows(values):
        flat = values.reshape(nodes * capacity, -1)
        return jnp.dot(picker, flat, precision=lax.Precision.HIGHEST)

    branch_state = (
        pick_rows(
            lax.all_to_all(
                state[0].reshape(nodes, items, drafts, heads),
                "req",
                split_axis=0,
                concat_axis=0,
                tiled=True,
            )
        ).reshape(rows, heads),
        pick_rows(
            lax.all_to_all(
                state[1].reshape(nodes, items, drafts, heads),
                "req",
                split_axis=0,
                concat_axis=0,
                tiled=True,
            )
        ).reshape(rows, heads),
        pick_rows(
            lax.all_to_all(
                state[2].reshape(nodes, items, drafts, width),
                "req",
                split_axis=0,
                concat_axis=0,
                tiled=True,
            )
        ).reshape(rows, heads, HD),
    )
    leaf_span = leaf_kv.shape[1]
    local_keys = jnp.concatenate(
        [leaf_kv[:, :, 0], own_keys.reshape(requests, drafts, width)], axis=1
    ).reshape(requests, leaf_span + drafts, heads, HD)
    local_values = jnp.concatenate(
        [leaf_kv[:, :, 1], own_values.reshape(requests, drafts, width)], axis=1
    ).reshape(requests, leaf_span + drafts, heads, HD)
    positions = jnp.arange(leaf_span + drafts)
    shifted = positions - leaf_span
    draft_pos = jnp.arange(drafts)
    local_usable = jnp.where(
        positions[None, None, :] < leaf_span,
        positions[None, None, :] < leaf_len[:, None, None],
        (shifted[None, None, :] <= draft_pos[None, :, None])
        & (shifted[None, None, :] < new_count[:, None, None]),
    )
    local_found = jax.vmap(partial_softmax)(
        queries.reshape(requests, drafts, heads, HD), local_keys, local_values, local_usable
    )
    local_state = (
        local_found[0].reshape(rows, heads),
        local_found[1].reshape(rows, heads),
        local_found[2].reshape(rows, heads, HD),
    )
    state = combine(combine(root_state, branch_state), local_state)
    attention = (state[2] / state[1][..., None]).reshape(rows, width).astype(jnp.bfloat16)
    terms = jnp.dot(attention, w_out, preferred_element_type=jnp.float32)
    summed = lax.psum_scatter(terms, "tensor", scatter_dimension=1, tiled=True)
    in_use = (draft_pos[None, :] < new_count[:, None]).reshape(rows)
    return jnp.where(in_use[:, None], summed, 0.0).astype(jnp.bfloat16)


def solution(mesh):
    placed = (
        P("req", None),
        P(),
        P(None, None, "tensor"),
        P("tensor", None),
        P("req", None, "tensor"),
        P("req", None, None, "tensor"),
        P("req", None, None, "tensor"),
        P("req", None),
        P(),
        P(),
        P("req"),
        P("req"),
    )
    return jax.shard_map(
        local, mesh=mesh, in_specs=placed, out_specs=P("req", "tensor"), check_vma=False
    )
```

profile of v0, /device:TPU:0, one launch (start us, length us, event | category | flops | bytes accessed | tf_op | source)
XLA Modules:
  0.0 132.0 jit_solution(8842183062406228737)
XLA Ops:
  7.3 4.7 %copy.105 = bf16[1024,3,512]{0,2,1:T(8,128)(2,1)} copy(bf16[1024,3,512]{2,0,1:T(8,128)(2,1)} %param.14) | data formatting | bytes 6291456 | tf_op args[2]
  12.2 3.0 %convolution_convert_fusion = bf16[64,1536]{1,0:T(8,128)(2,1)S(1)} fusion(bf16[1024,1536]{0,1:T(8,128)(2,1)} %bitcast.76, bf16[64,1024]{1,0:T(8,128)(2,1)S(1)} %copy-done.6, f32[1024]{0:T(1024)S(1)} %copy-done.13, f32[64]{0:T(128)S(1)} %add_rsqrt_fusion), kind=kOutput, calls=%fused_computation.7 | convolution fusion | flops 201687040 | bytes 3477760 | tf_op jit(solution)/shard_map/dot_general | solution.py:70
  17.2 7.4 %all-to-all-start = ((bf16[16,2,4,512]{3,2,1,0:T(4,128)(2,1)}), bf16[16,2,4,512]{3,2,1,0:T(4,128)(2,1)}, u32[]{:S(2)}, u32[]{:S(2)}) async-start(bf16[16,2,4,512]{3,2,1,0:T(4,128)(2,1)} %reshape.284), calls=%async_computation | async-start | bytes 262144 | tf_op jit(solution)/shard_map/all_to_all | solution.py:101
  25.5 4.2 %slice_reduce_fusion.1 = (bf16[16,16,512]{2,1,0:T(8,128)(2,1)S(1)}, bf16[16,16,512]{2,1,0:T(8,128)(2,1)}) fusion(bf16[16,16,2,512]{3,2,1,0:T(2,128)(2,1)} %param.18), kind=kLoop, calls=%fused_computation.38 | loop fusion | bytes 1048576 | tf_op jit(solution)/shard_map/slice | solution.py:146
  29.7 4.2 %fusion.73 = (bf16[1024,1,512]{2,1,0:T(2,128)(2,1)}, bf16[1024,1,512]{2,1,0:T(2,128)(2,1)}) fusion(bf16[1024,2,512]{2,1,0:T(2,128)(2,1)S(1)} %bitcast.77), kind=kLoop, calls=%fused_computation.105 | loop fusion | bytes 4194304 | tf_op jit(solution)/shard_map/slice | solution.py:107
  35.5 4.6 %copy.109 = bf16[1024,1,512]{0,2,1:T(8,128)(2,1)S(1)} copy(bf16[1024,1,512]{2,1,0:T(2,128)(2,1)} %get-tuple-element.12) | data formatting | bytes 2097152 | tf_op jit(solution)/shard_map/slice | solution.py:107
  43.4 2.2 %select_reduce_fusion = (f32[16,4,8]{1,2,0:T(8,128)S(1)}, f32[16,4,8,20]{3,1,2,0:T(4,128)}) fusion(pred[16,4,20]{2,1,0:T(4,128)(4,1)S(1)} %and_select_fusion, bf16[16,4,8,64]{3,2,1,0:T(8,128)(2,1)} %reshape.292, bf16[16,4,8,64]{3,1,2,0:T(4,128)(2,1)} %copy.118, bf16[16,16,8,64]{3,1,2,0:T(8,128)(2,1)S(1)} %copy.117), kind=kOutput, calls=%fused_computation.48 | convolution fusion | flops 1996288 | bytes 437504 | tf_op jit(solution)/shard_map/vmap(qhe,khe->qhk)/dot_general | solution.py:13
  45.6 1.1 reshape.285
  47.5 1.9 %copy-done.1 = f32[8,128,1024]{2,1,0:T(8,128)} copy-done((f32[8,128,1024]{2,1,0:T(8,128)}, f32[8,128,1024]{2,1,0:T(8,128)S(1)}, u32[]{:S(2)}) %copy-start.1) | copy-done | bytes 4194328
  49.4 1.0 fusion.3
  51.2 6.0 %all-to-all-start.3 = ((f32[16,2,4,8]{3,2,1,0:T(4,128)}), f32[16,2,4,8]{3,2,1,0:T(4,128)S(1)}, u32[]{:S(2)}, u32[]{:S(2)}) async-start(f32[16,2,4,8]{3,2,1,0:T(4,128)} %bitcast.16), calls=%async_computation.3 | async-start | bytes 131072 | tf_op jit(solution)/shard_map/all_to_all | solution.py:126
  57.2 2.2 %convolution_bitcast_fusion = f32[16,4,8,64]{3,1,2,0:T(4,128)} fusion(bf16[16,4,8,64]{3,1,2,0:T(4,128)(2,1)S(1)} %copy-done.12, bf16[16,16,8,64]{3,1,2,0:T(8,128)(2,1)} %copy.122, f32[16,4,8,20]{3,1,2,0:T(4,128)} %get-tuple-element.26, f32[16,4,8]{1,2,0:T(8,128)S(1)} %get-tuple-element.25, pred[16,4,20]{2,1,0:T(4,128)(4,1)S(1)} %and_select_fusion), kind=kOutput, calls=%fused_computation.17 | convolution fusion | flops 1996800 | bytes 503040 | tf_op jit(solution)/shard_map/vmap(qhk,khe->qhe)/dot_general | solution.py:20
  59.4 4.3 %copy.113 = bf16[1024,1,512]{0,2,1:T(8,128)(2,1)} copy(bf16[1024,1,512]{2,1,0:T(2,128)(2,1)S(1)} %copy-done.3) | data formatting | bytes 2097152 | tf_op jit(solution)/shard_map/slice | solution.py:107
  64.4 6.0 %all-to-all-start.1 = ((f32[16,2,4,8]{3,2,1,0:T(4,128)}), f32[16,2,4,8]{3,2,1,0:T(4,128)S(1)}, u32[]{:S(2)}, u32[]{:S(2)}) async-start(f32[16,2,4,8]{3,2,1,0:T(4,128)} %bitcast.9), calls=%async_computation.1 | async-start | bytes 131072 | tf_op jit(solution)/shard_map/all_to_all | solution.py:117
  70.5 3.5 %fusion.11 = f32[128,8,64]{0,2,1:T(8,128)S(1)} fusion(bf16[1024,8,64]{0,2,1:T(8,128)(2,1)} %bitcast.81, f32[8,128,1024]{2,1,0:T(8,128)} %copy-done.1, f32[128,8]{0,1:T(8,128)S(1)} %get-tuple-element.23, pred[1024]{0:T(1024)(128)(4,1)S(1)} %iota_compare_fusion.9), kind=kOutput, calls=%fused_computation.16 | convolution fusion | flops 138412032 | bytes 5510144 | tf_op jit(solution)/shard_map/qhk,khe->qhe/dot_general | solution.py:20
  75.1 2.2 %all-to-all-done.1 = f32[16,2,4,8]{3,2,1,0:T(4,128)S(1)} async-done(((f32[16,2,4,8]{3,2,1,0:T(4,128)}), f32[16,2,4,8]{3,2,1,0:T(4,128)S(1)}, u32[]{:S(2)}, u32[]{:S(2)}) %all-to-all-start.1) | async-done | bytes 4128 | tf_op jit(solution)/shard_map/all_to_all | solution.py:117
  77.4 3.8 %all-to-all-start.2 = ((f32[16,2,4,512]{3,2,1,0:T(4,128)}), f32[16,2,4,512]{3,2,1,0:T(4,128)S(1)}, u32[]{:S(2)}, u32[]{:S(2)}) async-start(f32[16,2,4,512]{3,2,1,0:T(4,128)} %reshape.289), calls=%async_computation.2 | async-start | bytes 524288 | tf_op jit(solution)/shard_map/all_to_all | solution.py:135
  84.0 7.2 %all-to-all-done.2 = f32[16,2,4,512]{3,2,1,0:T(4,128)S(1)} async-done(((f32[16,2,4,512]{3,2,1,0:T(4,128)}), f32[16,2,4,512]{3,2,1,0:T(4,128)S(1)}, u32[]{:S(2)}, u32[]{:S(2)}) %all-to-all-start.2) | async-done | bytes 262176 | tf_op jit(solution)/shard_map/all_to_all | solution.py:135
  92.3 6.4 %fusion.74 = (bf16[1024,1,512]{2,1,0:T(2,128)(2,1)S(1)}, bf16[1024,1,512]{2,1,0:T(2,128)(2,1)}) fusion(bf16[1024,2,512]{2,1,0:T(2,128)(2,1)} %all-gather.2.cloned.1.call-done), kind=kLoop, calls=%fused_computation.106 | loop fusion | bytes 4194304 | tf_op jit(solution)/shard_map/slice | solution.py:80
  98.8 5.8 %copy.108 = bf16[1024,1,512]{0,2,1:T(8,128)(2,1)} copy(bf16[1024,1,512]{2,1,0:T(2,128)(2,1)} %get-tuple-element.15) | data formatting | bytes 2097152 | tf_op jit(solution)/shard_map/slice | solution.py:80
  104.6 4.2 %copy.106 = bf16[1024,1,512]{0,2,1:T(8,128)(2,1)} copy(bf16[1024,1,512]{2,1,0:T(2,128)(2,1)S(1)} %get-tuple-element.14) | data formatting | bytes 2097152 | tf_op jit(solution)/shard_map/slice | solution.py:80
  108.8 1.8 %bitcast_reduce_fusion = (f32[64,8]{0,1:T(8,128)S(1)}, f32[8,64,1024]{2,1,0:T(8,128)S(1)}) fusion(bf16[1024,8,64]{0,2,1:T(8,128)(2,1)} %bitcast.78, bf16[64,8,64]{2,1,0:T(8,128)(2,1)S(1)} %reshape.282), kind=kOutput, calls=%fused_computation.10 | convolution fusion | flops 68156928 | bytes 3213312 | tf_op jit(solution)/shard_map/qhe,khe->qhk/dot_general | solution.py:13
  113.6 10.0 %reduce-scatter.2.cloned.1.call-done = f32[64,512]{1,0:T(8,128)} async-done(((f32[64,1024]{1,0:T(8,128)}), f32[64,512]{1,0:T(8,128)}) %reduce-scatter.2.cloned.1.call-update) | async-done | bytes 131088 | tf_op jit(solution)/shard_map/reduce_scatter | solution.py:171
  123.6 1.6 %select_convert_fusion = bf16[64,512]{1,0:T(8,128)(2,1)} fusion(f32[64,512]{1,0:T(8,128)} %reduce-scatter.2.cloned.1.call-done, pred[64]{0:T(512)(128)(4,1)S(1)} %lt.89), kind=kLoop, calls=%fused_computation.54 | loop fusion | flops 32768 | bytes 196672 | tf_op jit(solution)/shard_map/convert_element_type | solution.py:173
  (102 shorter events, 18.7 us)
Async XLA Ops:
  6.5 105.9 %copy-start = (bf16[512,1024]{1,0:T(8,128)(2,1)S(1)}, bf16[512,1024]{1,0:T(8,128)(2,1)}, u32[]{:S(2)}) copy-start(bf16[512,1024]{1,0:T(8,128)(2,1)} %param.15) | copy-start | bytes 3145732
  6.5 85.8 %all-gather.2.cloned.1.call-start = ((), (), s32[]{:S(2)}) async-start(), calls=%async_computation.5 | async-start | bytes 2228224 | tf_op jit(solution)/shard_map/all_gather | solution.py:77
  7.3 4.8 %copy-start.6 = (bf16[64,1024]{1,0:T(8,128)(2,1)S(1)}, bf16[64,1024]{1,0:T(8,128)(2,1)}, u32[]{:S(2)}) copy-start(bf16[64,1024]{1,0:T(8,128)(2,1)} %param.12) | copy-start | bytes 393220
  7.3 4.9 %copy-start.13 = (f32[1024]{0:T(1024)S(1)}, f32[1024]{0:T(1024)}, u32[]{:S(2)}) copy-start(f32[1024]{0:T(1024)} %param.13) | copy-start | bytes 12292
  12.0 3.9 %copy-start.17 = (s32[16]{0:T(128)S(1)}, s32[16]{0:T(128)}, u32[]{:S(2)}) copy-start(s32[16]{0:T(128)} %param.20) | copy-start | bytes 196
  12.0 3.9 %copy-start.19 = (s32[16,1]{0,1:T(1,128)S(1)}, s32[16,1]{0,1:T(1,128)}, u32[]{:S(2)}) copy-start(s32[16,1]{0,1:T(1,128)} %param.19) | copy-start | bytes 196
  12.2 12.5 %copy-start.16 = (s32[16]{0:T(128)S(1)}, s32[16]{0:T(128)}, u32[]{:S(2)}) copy-start(s32[16]{0:T(128)} %param.21) | copy-start | bytes 196
  12.2 13.2 %copy-start.14 = (s32[16]{0:T(128)S(1)}, s32[16]{0:T(128)}, u32[]{:S(2)}) copy-start(s32[16]{0:T(128)} %param.23) | copy-start | bytes 196
  12.2 13.2 %copy-start.18 = (s32[16]{0:T(128)S(1)}, s32[16]{0:T(128)}, u32[]{:S(2)}) copy-start(s32[16]{0:T(128)} %param.22) | copy-start | bytes 196
  15.2 14.5 %copy-start.2 = (bf16[1,1024,2,512]{3,2,1,0:T(2,128)(2,1)S(1)}, bf16[1,1024,2,512]{3,2,1,0:T(2,128)(2,1)}, u32[]{:S(2)}) copy-start(bf16[1,1024,2,512]{3,2,1,0:T(2,128)(2,1)} %param.17) | copy-start | bytes 6291460
  17.2 28.4 %all-to-all-start = ((bf16[16,2,4,512]{3,2,1,0:T(4,128)(2,1)}), bf16[16,2,4,512]{3,2,1,0:T(4,128)(2,1)}, u32[]{:S(2)}, u32[]{:S(2)}) async-start(bf16[16,2,4,512]{3,2,1,0:T(4,128)(2,1)} %reshape.284), calls=%async_computation | async-start | bytes 262144 | tf_op jit(solution)/shard_map/all_to_all | solution.py:101
  33.9 6.1 %copy-start.11 = (bf16[64,512]{1,0:T(8,128)(2,1)S(1)}, bf16[64,512]{1,0:T(8,128)(2,1)}, u32[]{:S(2)}) copy-start(bf16[64,512]{1,0:T(8,128)(2,1)} %get-tuple-element.17) | copy-start | bytes 196612
  33.9 7.0 %copy-start.5 = (bf16[16,16,512]{2,1,0:T(8,128)(2,1)S(1)}, bf16[16,16,512]{2,1,0:T(8,128)(2,1)}, u32[]{:S(2)}) copy-start(bf16[16,16,512]{2,1,0:T(8,128)(2,1)} %get-tuple-element.6) | copy-start | bytes 786436
  49.4 7.7 %copy-start.12 = (bf16[16,4,8,64]{3,1,2,0:T(4,128)(2,1)S(1)}, bf16[16,4,8,64]{3,1,2,0:T(4,128)(2,1)}, u32[]{:S(2)}) copy-start(bf16[16,4,8,64]{3,1,2,0:T(4,128)(2,1)} %copy.123) | copy-start | bytes 196612
  50.4 9.0 %copy-start.3 = (bf16[1024,1,512]{2,1,0:T(2,128)(2,1)S(1)}, bf16[1024,1,512]{2,1,0:T(2,128)(2,1)}, u32[]{:S(2)}) copy-start(bf16[1024,1,512]{2,1,0:T(2,128)(2,1)} %get-tuple-element.13) | copy-start | bytes 3145732
  51.2 13.3 %all-to-all-start.3 = ((f32[16,2,4,8]{3,2,1,0:T(4,128)}), f32[16,2,4,8]{3,2,1,0:T(4,128)S(1)}, u32[]{:S(2)}, u32[]{:S(2)}) async-start(f32[16,2,4,8]{3,2,1,0:T(4,128)} %bitcast.16), calls=%async_computation.3 | async-start | bytes 131072 | tf_op jit(solution)/shard_map/all_to_all | solution.py:126
  64.4 12.9 %all-to-all-start.1 = ((f32[16,2,4,8]{3,2,1,0:T(4,128)}), f32[16,2,4,8]{3,2,1,0:T(4,128)S(1)}, u32[]{:S(2)}, u32[]{:S(2)}) async-start(f32[16,2,4,8]{3,2,1,0:T(4,128)} %bitcast.9), calls=%async_computation.1 | async-start | bytes 131072 | tf_op jit(solution)/shard_map/all_to_all | solution.py:117
  74.0 7.4 %copy-start.9 = (f32[16,4,8,20]{3,1,2,0:T(4,128)S(1)}, f32[16,4,8,20]{3,1,2,0:T(4,128)}, u32[]{:S(2)}) copy-start(f32[16,4,8,20]{3,1,2,0:T(4,128)} %get-tuple-element.26) | copy-start | bytes 122884
  74.0 8.1 %copy-start.10 = (f32[16,4,8,64]{3,1,2,0:T(4,128)S(1)}, f32[16,4,8,64]{3,1,2,0:T(4,128)}, u32[]{:S(2)}) copy-start(f32[16,4,8,64]{3,1,2,0:T(4,128)} %convolution_bitcast_fusion) | copy-start | bytes 393220
  77.4 13.8 %all-to-all-start.2 = ((f32[16,2,4,512]{3,2,1,0:T(4,128)}), f32[16,2,4,512]{3,2,1,0:T(4,128)S(1)}, u32[]{:S(2)}, u32[]{:S(2)}) async-start(f32[16,2,4,512]{3,2,1,0:T(4,128)} %reshape.289), calls=%async_computation.2 | async-start | bytes 524288 | tf_op jit(solution)/shard_map/all_to_all | solution.py:135
  81.1 42.4 %reduce-scatter.2.cloned.1.call-start = ((), (), s32[]{:S(2)}) async-start(), calls=%async_computation.6 | async-start | bytes 393216 | tf_op jit(solution)/shard_map/reduce_scatter | solution.py:171
  108.8 2.4 %copy-start.4 = (bf16[1024,1,512]{0,2,1:T(8,128)(2,1)S(1)}, bf16[1024,1,512]{0,2,1:T(8,128)(2,1)}, u32[]{:S(2)}) copy-start(bf16[1024,1,512]{0,2,1:T(8,128)(2,1)} %copy.108) | copy-start | bytes 3145732
  108.8 2.4 %copy-start.7 = (f32[64,8,64]{2,1,0:T(8,128)S(1)}, f32[64,8,64]{2,1,0:T(8,128)}, u32[]{:S(2)}) copy-start(f32[64,8,64]{2,1,0:T(8,128)} %reshape.291) | copy-start | bytes 393220
  108.8 2.4 %copy-start.8 = (f32[16,4,8,64]{3,1,0,2:T(4,128)S(1)}, f32[16,4,8,64]{3,1,0,2:T(4,128)}, u32[]{:S(2)}) copy-start(f32[16,4,8,64]{3,1,0,2:T(4,128)} %copy.124) | copy-start | bytes 393220
  (2 other events, 3.2 us)
Sparse Core Ops, SparseCore 0:
  9.5 46.0 all-gather.1
  113.5 9.9 reduce-scatter.1
where the time goes:
time: 133 us; the launch traced here: 132 us
  local copies, waits for them, and re-layouts  52.8 us (40%)
  starting transfers between devices  23.4 us (18%)
  waiting for transfers between devices  20.1 us (15%)
  matrix products  16.3 us (12%)
  between operations  13.8 us (10%)
  other arithmetic  5.72 us (4%)
    slice x2, local copies, waits for them, and re-layouts, local(): piece[:, 0].reshape(-1, heads, HD)  10.6 us
    reduce_scatter x1, waiting for transfers between devices, local(): summed = lax.psum_scatter(terms, 'tensor', scatter_dimension=1, tiled=True)  9.98 us
    slice x2, local copies, waits for them, and re-layouts, local(): cache[:, 0].reshape(span, heads, HD)  8.78 us
    all_to_all x1, starting transfers between devices, local(): lax.all_to_all(outgoing, 'req', split_axis=0, concat_axis=0, tiled=True)  7.41 us
    all_to_all x1, waiting for transfers between devices, local(): lax.all_to_all(state[2].reshape(nodes, items, drafts, width), 'req', spli...  7.15 us
    unnamed x42, local copies, waits for them, and re-layouts  6.85 us
    dot_general x3, matrix products, partial_softmax(): jnp.einsum('qhk,khe->qhe', weights.astype(jnp.bfloat16), value_rows, pref...  6.65 us
    all_to_all x1, starting transfers between devices, local(): lax.all_to_all(state[0].reshape(nodes, items, drafts, heads), 'req', spli...  6.01 us
  transfers between devices with their start and end apart: 6, of which 3 were waited for; matrix products, arithmetic and copies ran while one was open for 38% of the time, Pallas kernels for 0%

commit v1 on v0

v1 whole, which is shorter than its diff:
```python
import functools
import math

import jax
import jax.numpy as jnp
from jax import lax
from jax.experimental import pallas as pl
from jax.experimental.pallas import tpu as pltpu
from jax.sharding import PartitionSpec as P

HD = 64
MESH = pl.DeviceIdType.MESH
F32 = jnp.float32
BF16 = jnp.bfloat16
SCALE = HD ** (-0.5) * math.log2(math.e)
LOG2E = math.log2(math.e)


def iota(shape, dim):
    return lax.broadcasted_iota(jnp.int32, shape, dim)


def dot(a, b):
    return jnp.dot(a, b, preferred_element_type=F32)


def dot_t(a, b):
    return lax.dot_general(a, b, (((1,), (1,)), ((), ())), preferred_element_type=F32)


def kernel(
    n, nt, drafts, cap,
    tok_ref, gain_ref, w_hbm, wout_hbm, root_ref, bkv_hbm, leaf_hbm,
    branch_ref, owner_ref, blen_ref, llen_ref, newc_ref,
    out_ref,
    w_ref, wout_ref, braw, lraw, kroot, vroot, kbr, vbr, kloc, vloc,
    oq, aq, bo, br, tb, tr, sbuf, pbuf, peak_buf, sum_buf, asked,
    local_sem, ring_send, ring_recv, sib_send, sib_recv,
    q_send, q_recv, b_send, b_recv, t_send, t_recv,
):
    rows = tok_ref.shape[0]
    requests = rows // drafts
    width = wout_hbm.shape[0]
    gw = min(width, 256)
    hg = gw // HD
    groups = width // gw
    cd = cap * drafts
    slot = oq.shape[1]
    span = bkv_hbm.shape[0]
    leaf_span = leaf_hbm.shape[0] // requests
    block = root_ref.shape[0]
    chips = n // 2
    half = chips // 2
    me = lax.axis_index("req")
    tn = lax.axis_index("tensor")

    loads = [pltpu.make_async_copy(w_hbm.at[j], w_ref.at[j], local_sem.at[j]) for j in range(3)]
    loads.append(pltpu.make_async_copy(bkv_hbm, braw, local_sem.at[3]))
    loads.append(pltpu.make_async_copy(leaf_hbm, lraw, local_sem.at[4]))
    loads.append(pltpu.make_async_copy(wout_hbm, wout_ref, local_sem.at[5]))
    for load in loads:
        load.start()

    barrier = pltpu.get_barrier_semaphore()

    def greet(j, carry):
        pl.semaphore_signal(
            barrier, inc=1, device_id=(lax.rem(me + j, n), tn), device_id_type=MESH
        )
        return carry

    lax.fori_loop(1, n, greet, 0)
    for j in range(1, nt):
        pl.semaphore_signal(
            barrier, inc=1, device_id=(me, lax.rem(tn + j, nt)), device_id_type=MESH
        )

    def split_rows(raw, count):
        pick = iota((2 * count, 2 * count), 0)
        col = iota((2 * count, 2 * count), 1)
        source = jnp.where(pick < count, 2 * pick, 2 * (pick - count) + 1)
        parted = dot((col == source).astype(BF16), raw).astype(BF16)
        return parted[:count], parted[count:]

    own_k, own_v = split_rows(root_ref.reshape(2 * block, width)[...], block)
    kroot[me] = own_k
    vroot[me] = own_v

    pl.semaphore_wait(barrier, n - 1 + nt - 1)

    core = lax.rem(me, 2)
    chip = lax.div(me, 2)
    zc = lax.div(chip, 2)
    xc = lax.rem(chip, 2)
    place = (1 - xc) * zc + xc * (2 * half - 1 - zc)

    def device_at(position):
        q = lax.rem(position + 2 * chips, chips)
        xq = lax.div(q, half)
        zq = (1 - xq) * q + xq * (2 * half - 1 - q)
        return (zq * 2 + xq) * 2 + core

    sibling = me + 1 - 2 * core
    stores = (kroot, vroot)

    def ring(direction, hop, j, outgoing):
        sign = 1 - 2 * direction
        origin = device_at(place - sign * (hop - 1 if outgoing else hop))
        return pltpu.make_async_remote_copy(
            src_ref=stores[j].at[origin], dst_ref=stores[j].at[origin],
            send_sem=ring_send.at[direction, hop, j], recv_sem=ring_recv.at[direction, hop, j],
            device_id=(device_at(place + sign), tn), device_id_type=MESH,
        )

    def share(index, offset, j, outgoing):
        origin = device_at(place + offset)
        if not outgoing:
            origin = origin + 1 - 2 * core
        return pltpu.make_async_remote_copy(
            src_ref=stores[j].at[origin], dst_ref=stores[j].at[origin],
            send_sem=sib_send.at[index, j], recv_sem=sib_recv.at[index, j],
            device_id=(sibling, tn), device_id_type=MESH,
        )

    def travels(direction, hop, j):
        return hop < half or (hop == half and j == direction)

    sent = []
    shared = []

    def send_on(direction, hop, j):
        if travels(direction, hop, j):
            copy = ring(direction, hop, j, True)
            copy.start()
            sent.append(copy)

    def send_share(index, offset, j):
        copy = share(index, offset, j, True)
        copy.start()
        sent.append(copy)
        shared.append((index, offset, j))

    def pump(hop):
        for j in range(2):
            for direction in range(2):
                if travels(direction, hop, j):
                    ring(direction, hop, j, False).wait_recv()
                    send_on(direction, hop + 1, j)
                    offset = -hop if direction == 0 else hop
                    send_share(direction * half + hop, offset, j)

    for j in range(2):
        for direction in range(2):
            send_on(direction, 1, j)
    for j in range(2):
        send_share(0, 0, j)

    floats = tok_ref[...].astype(F32)
    mean = jnp.mean(floats * floats, axis=1, keepdims=True)
    normed = (floats * lax.rsqrt(mean + 1e-05) * gain_ref[...]).astype(BF16)
    loads[0].wait()
    queries = dot(normed, w_ref[0]).astype(BF16)

    row_req = lax.div(iota((rows, requests), 0), drafts)
    at_req = row_req == iota((rows, requests), 1)

    def per_row(values):
        return jnp.sum(jnp.where(at_req, values.astype(F32), 0.0), axis=1, keepdims=True)

    node_of = per_row(branch_ref[...])
    chosen = (node_of == iota((rows, n), 1).astype(F32)).astype(BF16)
    owners = (owner_ref[...] == iota((n, n), 0)).astype(BF16)
    target = dot_t(chosen, owners).astype(BF16)
    target_t = dot_t(owners, chosen).astype(BF16)
    same = dot_t(target, target)
    ri, rj = iota((rows, rows), 0), iota((rows, rows), 1)
    qi, qj = lax.div(ri, drafts), lax.div(rj, drafts)
    first_j = lax.rem(rj, drafts) == 0
    first_i = lax.rem(ri, drafts) == 0
    order_col = jnp.sum(jnp.where((qj < qi) & first_j, same, 0.0), axis=1, keepdims=True)
    order_row = jnp.sum(jnp.where((qi < qj) & first_i, same, 0.0), axis=0, keepdims=True)
    total = n * slot
    spread = (lax.div(iota((total, n), 0), slot) == iota((total, n), 1)).astype(BF16)

    def slot_parts(shape, dim):
        inner = lax.rem(iota(shape, dim), slot)
        item = lax.rem(inner, cd)
        return lax.div(inner, cd), lax.div(item, drafts).astype(F32), lax.rem(item, drafts)

    group_k, item_k, draft_k = slot_parts((total, rows), 0)
    put = (dot(spread, target_t) > 0.5) & (order_row == item_k) & (
        lax.rem(iota((total, rows), 1), drafts) == draft_k
    )
    packed = jnp.zeros((total, gw), F32)
    for g in range(groups):
        mine = jnp.where(put & (group_k == g), 1.0, 0.0).astype(BF16)
        packed = packed + dot(mine, queries[:, g * gw : (g + 1) * gw])
    oq[...] = packed.astype(BF16).reshape(n, slot, gw)
    aq[me] = oq[me]

    def exchange(source, landing, send_sem, recv_sem, j, outgoing):
        there = lax.rem(me + j, n)
        here = me if outgoing else lax.rem(me + n - j, n)
        return pltpu.make_async_remote_copy(
            src_ref=source.at[there], dst_ref=landing.at[here],
            send_sem=send_sem.at[j], recv_sem=recv_sem.at[j],
            device_id=(there, tn), device_id_type=MESH,
        )

    for j in range(1, n):
        exchange(oq, aq, q_send, q_recv, j, True).start()

    pump(1)

    loads[1].wait()
    own_keys = dot(normed, w_ref[1]).astype(BF16)
    loads[2].wait()
    own_values = dot(normed, w_ref[2]).astype(BF16)

    loads[3].wait()
    piece = min(128, span)
    braw_rows = braw.reshape(2 * span, width)

    def part_branch(b, carry):
        raw = braw_rows[pl.ds(pl.multiple_of(2 * piece * b, 2 * piece), 2 * piece), :]
        k_part, v_part = split_rows(raw, piece)
        at = pl.ds(pl.multiple_of(piece * b, piece), piece)
        kbr[at, :] = k_part
        vbr[at, :] = v_part
        return carry

    lax.fori_loop(0, span // piece, part_branch, 0)

    if half >= 2:
        pump(2)

    col_head = lax.div(iota((1, gw), 1), HD)

    def stack(part):
        return jnp.concatenate(
            [jnp.where(col_head == h, part, 0.0) for h in range(hg)], axis=0
        ).astype(BF16)

    def attend(scores, mask, values):
        peaks, sums, weights = [], [], []
        for s, keep in zip(scores, mask):
            if keep is not None:
                s = jnp.where(keep, s, -1e30)
            peak = jnp.max(s, axis=1, keepdims=True)
            w = jnp.exp2((s - peak) * SCALE)
            peaks.append(peak)
            sums.append(jnp.sum(w, axis=1, keepdims=True))
            weights.append(w.astype(BF16))
        weighted = dot(jnp.concatenate(weights, axis=0), values)
        return peaks, sums, weighted

    def attend_long(stacked_rows, keys_of, values_of, keep, step):
        amount_of, length = stacked_rows.shape[0], keys_of.shape[0]
        sbuf[:amount_of, :length] = dot_t(stacked_rows, keys_of)

        def some(c, carry):
            at = pl.ds(pl.multiple_of(c * step, step), step)
            s = sbuf[at, :length]
            if keep is not None:
                s = jnp.where(keep, s, -1e30)
            peak = jnp.max(s, axis=1, keepdims=True)
            w = jnp.exp2((s - peak) * SCALE)
            peak_buf[at, :] = jnp.broadcast_to(peak, (step, 128))
            sum_buf[at, :] = jnp.broadcast_to(jnp.sum(w, axis=1, keepdims=True), (step, 128))
            pbuf[at, :length] = w.astype(BF16)
            return carry

        lax.fori_loop(0, amount_of // step, some, 0)
        weighted = dot(pbuf[:amount_of, :length], values_of)
        return peak_buf[:amount_of, :1], sum_buf[:amount_of, :1], weighted

    for j in range(1, n):
        exchange(oq, aq, q_send, q_recv, j, False).wait_recv()
    asked[...] = aq[...].astype(F32)
    owned = jnp.sum(
        jnp.where(owner_ref[...] == me, blen_ref[...], 0).astype(F32), axis=1, keepdims=True
    )
    usable = iota((1, span), 1).astype(F32) < owned
    count = n * cd
    lane = iota((1, 128), 1)
    slabs = []
    for g in range(groups):
        part = asked[:, g * cd : (g + 1) * cd, :].reshape(count, gw)
        cols = slice(g * gw, (g + 1) * gw)
        peaks, sums, weighted = attend_long(stack(part), kbr[:, cols], vbr[:, cols], usable, 128)
        inverse = 1.0 / sums
        level = peaks * SCALE + jnp.log(sums) * LOG2E
        mixed = jnp.zeros((count, gw), F32)
        levels = jnp.zeros((count, 128), F32)
        for h in range(hg):
            at = slice(h * count, (h + 1) * count)
            mixed = jnp.where(col_head == h, weighted[at] * inverse[at], mixed)
            levels = jnp.where(lax.rem(lane, hg) == h, level[at], levels)
        high = levels.astype(BF16).astype(F32)
        middle = (levels - high).astype(BF16).astype(F32)
        low = levels - high - middle
        stats = jnp.where(lane < hg, high, jnp.where(lane < 2 * hg, middle, low))
        stats = jnp.where(lane < 3 * hg, stats, 0.0)
        slabs.append(jnp.concatenate([mixed, stats], axis=1).reshape(n, cd, gw + 128))
        if half >= 3 and g == 0:
            pump(3)
    if groups * cd < slot:
        slabs.append(jnp.zeros((n, slot - groups * cd, gw + 128), F32))
    bo[...] = jnp.concatenate(slabs, axis=1).astype(BF16)
    br[me] = bo[me]
    for j in range(1, n):
        exchange(bo, br, b_send, b_recv, j, True).start()

    loads[4].wait()
    leaf_rows = requests * leaf_span
    lpiece = min(128, leaf_rows)
    lraw_rows = lraw.reshape(2 * leaf_rows, width)

    def part_leaf(b, carry):
        raw = lraw_rows[pl.ds(pl.multiple_of(2 * lpiece * b, 2 * lpiece), 2 * lpiece), :]
        k_part, v_part = split_rows(raw, lpiece)
        at = pl.ds(pl.multiple_of(lpiece * b, lpiece), lpiece)
        kloc[at, :] = k_part
        vloc[at, :] = v_part
        return carry

    lax.fori_loop(0, leaf_rows // lpiece, part_leaf, 0)
    kloc[pl.ds(leaf_rows, rows), :] = own_keys
    vloc[pl.ds(leaf_rows, rows), :] = own_values
    keys = leaf_rows + rows
    leaf_len = per_row(llen_ref[...])
    new_count = per_row(newc_ref[...])
    ki, kj = iota((rows, keys), 0), iota((rows, keys), 1)
    own_j = kj - leaf_rows
    draft_j = lax.rem(jnp.maximum(own_j, 0), drafts)
    in_leaf = (
        (lax.div(kj, leaf_span) == lax.div(ki, drafts))
        & (lax.rem(kj, leaf_span).astype(F32) < leaf_len)
    )
    in_own = (
        (lax.div(jnp.maximum(own_j, 0), drafts) == lax.div(ki, drafts))
        & (draft_j <= lax.rem(ki, drafts))
        & (draft_j.astype(F32) < new_count)
    )
    local_keep = ((kj < leaf_rows) & in_leaf) | ((kj >= leaf_rows) & in_own)
    stacked = [stack(queries[:, g * gw : (g + 1) * gw].astype(F32)) for g in range(groups)]
    local_states = []
    for g in range(groups):
        cols = slice(g * gw, (g + 1) * gw)
        scores = dot_t(stacked[g], kloc[:, cols])
        pieces = [scores[h * rows : (h + 1) * rows] for h in range(hg)]
        local_states.append(attend(pieces, [local_keep] * hg, vloc[:, cols]))

    for hop in range(1 if half < 2 else 4 if half >= 3 else 3, half + 1):
        if hop > 1:
            pump(hop)
    for index, offset, j in shared:
        share(index, offset, j, False).wait_recv()

    before = []
    for g in range(groups):
        cols = slice(g * gw, (g + 1) * gw)
        root_keys = kroot[:, :, cols].reshape(n * block, gw)
        root_values = vroot[:, :, cols].reshape(n * block, gw)
        peaks, sums, weighted = attend_long(stacked[g], root_keys, root_values, None, rows)
        lpeaks, lsums, lweighted = local_states[g]
        level = jnp.zeros((rows, gw), F32)
        amount = jnp.zeros((rows, gw), F32)
        mixed = jnp.zeros((rows, gw), F32)
        for h in range(hg):
            at = slice(h * rows, (h + 1) * rows)
            top = jnp.maximum(peaks[at], lpeaks[h])
            one = jnp.exp2((peaks[at] - top) * SCALE)
            two = jnp.exp2((lpeaks[h] - top) * SCALE)
            level = jnp.where(col_head == h, top * SCALE, level)
            amount = jnp.where(col_head == h, one * sums[at] + two * lsums[h], amount)
            mixed = jnp.where(col_head == h, one * weighted[at] + two * lweighted[at], mixed)
        before.append((level, amount, mixed))

    group_l, item_l, draft_l = slot_parts((rows, total), 1)
    take = (dot_t(target, spread) > 0.5) & (order_col == item_l) & (
        lax.rem(iota((rows, total), 0), drafts) == draft_l
    )
    takes = [jnp.where(take & (group_l == g), 1.0, 0.0).astype(BF16) for g in range(groups)]
    loads[5].wait()

    for j in range(1, n):
        exchange(bo, br, b_send, b_recv, j, False).wait_recv()
    flat = br[...].reshape(total, gw + 128)
    heads = []
    for g in range(groups):
        got = dot(takes[g], flat)
        stats = got[:, gw:]
        level, amount, mixed = before[g]
        other = jnp.zeros((rows, gw), F32)
        for h in range(hg):
            joined = (
                stats[:, h : h + 1]
                + stats[:, hg + h : hg + h + 1]
                + stats[:, 2 * hg + h : 2 * hg + h + 1]
            )
            other = jnp.where(col_head == h, joined, other)
        top = jnp.maximum(level, other)
        one = jnp.exp2(level - top)
        two = jnp.exp2(other - top)
        heads.append(((one * mixed + two * got[:, :gw]) / (one * amount + two)).astype(BF16))
    attention = heads[0] if groups == 1 else jnp.concatenate(heads, axis=1)
    ow = out_ref.shape[1]
    for t in range(nt):
        tb[t] = dot(attention, wout_ref[:, t * ow : (t + 1) * ow])

    def reduce_copy(j, outgoing):
        there = lax.rem(tn + j, nt)
        here = tn if outgoing else lax.rem(tn + nt - j, nt)
        return pltpu.make_async_remote_copy(
            src_ref=tb.at[there], dst_ref=tr.at[here],
            send_sem=t_send.at[j], recv_sem=t_recv.at[j],
            device_id=(me, there), device_id_type=MESH,
        )

    for j in range(1, nt):
        reduce_copy(j, True).start()
    in_use = lax.rem(iota((rows, 1), 0), drafts).astype(F32) < new_count
    result = tb[tn]
    for copy in sent:
        copy.wait_send()
    for j in range(1, n):
        exchange(oq, aq, q_send, q_recv, j, True).wait_send()
        exchange(bo, br, b_send, b_recv, j, True).wait_send()
    for j in range(1, nt):
        reduce_copy(j, False).wait_recv()
        result = result + tr[lax.rem(tn + nt - j, nt)]
    out_ref[...] = jnp.where(in_use, result, 0.0).astype(BF16)
    for j in range(1, nt):
        reduce_copy(j, True).wait_send()


def local(
    n, nt,
    tokens, norm_gain, w_qkv, w_out, root_kv, branch_kv, leaf_kv,
    branch, node_owner, branch_len, leaf_len, new_count,
):
    rows, depth = tokens.shape
    requests = branch.shape[0]
    drafts = rows // requests
    nodes = node_owner.shape[0]
    width = w_out.shape[0]
    ow = w_out.shape[1] // nt
    cap = max(2, 2 * requests // nodes)
    gw = min(width, 256)
    slot = max(16, width // gw * cap * drafts)
    block = root_kv.shape[0]
    span = branch_kv.shape[1]
    leaf_rows = leaf_kv.shape[0] * leaf_kv.shape[1]
    half = n // 4
    long_rows = gw // HD * max(n * cap * drafts, rows)
    longest = max(span, n * block)
    vmem = pl.BlockSpec(memory_space=pltpu.VMEM)
    hbm = pl.BlockSpec(memory_space=pl.ANY)
    dma = pltpu.SemaphoreType.DMA
    return pl.pallas_call(
        functools.partial(kernel, n, nt, drafts, cap),
        out_shape=jax.ShapeDtypeStruct((rows, ow), BF16),
        in_specs=[vmem, vmem, hbm, hbm, vmem, hbm, hbm] + [vmem] * 5,
        out_specs=vmem,
        scratch_shapes=[
            pltpu.VMEM((3, depth, width), BF16),
            pltpu.VMEM(w_out.shape, BF16),
            pltpu.VMEM((span, 2, width), BF16),
            pltpu.VMEM((leaf_rows, 2, width), BF16),
            pltpu.VMEM((n, block, width), BF16),
            pltpu.VMEM((n, block, width), BF16),
            pltpu.VMEM((span, width), BF16),
            pltpu.VMEM((span, width), BF16),
            pltpu.VMEM((leaf_rows + rows, width), BF16),
            pltpu.VMEM((leaf_rows + rows, width), BF16),
            pltpu.VMEM((n, slot, gw), BF16),
            pltpu.VMEM((n, slot, gw), BF16),
            pltpu.VMEM((n, slot, gw + 128), BF16),
            pltpu.VMEM((n, slot, gw + 128), BF16),
            pltpu.VMEM((nt, rows, ow), F32),
            pltpu.VMEM((nt, rows, ow), F32),
            pltpu.VMEM((long_rows, longest), F32),
            pltpu.VMEM((long_rows, longest), BF16),
            pltpu.VMEM((long_rows, 128), F32),
            pltpu.VMEM((long_rows, 128), F32),
            pltpu.VMEM((n, slot, gw), F32),
            dma((6,)),
            dma((2, half + 1, 2)),
            dma((2, half + 1, 2)),
            dma((2 * half + 1, 2)),
            dma((2 * half + 1, 2)),
            dma((n,)),
            dma((n,)),
            dma((n,)),
            dma((n,)),
            dma((nt,)),
            dma((nt,)),
        ],
        compiler_params=pltpu.CompilerParams(
            collective_id=0, has_side_effects=True, vmem_limit_bytes=58 << 20
        ),
    )(
        tokens,
        norm_gain.reshape(1, -1),
        jnp.transpose(w_qkv, (1, 0, 2)),
        w_out,
        root_kv,
        branch_kv.reshape(span, 2, width),
        leaf_kv.reshape(leaf_rows, 2, width),
        branch.reshape(1, requests),
        node_owner.reshape(1, nodes),
        branch_len.reshape(1, nodes),
        leaf_len.reshape(1, requests),
        new_count.reshape(1, requests),
    )


def solution(mesh):
    placed = (
        P("req", None),
        P(),
        P(None, None, "tensor"),
        P("tensor", None),
        P("req", None, "tensor"),
        P("req", None, None, "tensor"),
        P("req", None, None, "tensor"),
        P("req", None),
        P(),
        P(),
        P("req"),
        P("req"),
    )
    return jax.shard_map(
        functools.partial(local, mesh.shape["req"], mesh.shape["tensor"]),
        mesh=mesh, in_specs=placed, out_specs=P("req", "tensor"), check_vma=False,
    )
```

time: 133 us -> 36.6 us (0.28)
  local copies, waits for them, and re-layouts: 52.8 us -> 1.47 us
  Pallas kernels: 0 us -> 35 us
  starting transfers between devices: 23.4 us -> 0 us
  waiting for transfers between devices: 20.1 us -> 0 us
  matrix products: 16.3 us -> 0 us
  between operations: 13.8 us -> 0.01 us
  other arithmetic: 5.72 us -> 0 us
    pallas_call x0 -> x1, Pallas kernels: none -> 35 us  [local(): pl.pallas_call(functools.partial(kernel, n, nt, drafts, cap), out_shape=j...]
    slice x8 -> x0, local copies, waits for them, and re-layouts: 34.4 us -> none  [the longest x2 10.6 us: local(): piece[:, 0].reshape(-1, heads, HD)]
    all_to_all x4 -> x0, starting transfers between devices: 23.2 us -> none  [the longest x1 7.41 us: local(): lax.all_to_all(outgoing, 'req', split_axis=0, concat_axis=0, tiled=True)]
    dot_general x12 -> x0, matrix products: 16.3 us -> none  [the longest x3 6.65 us: partial_softmax(): jnp.einsum('qhk,khe->qhe', weights.astype(jnp.bfloat16), value_rows, pref...]
    reduce_scatter x1 -> x0, waiting for transfers between devices: 9.98 us -> none  [local(): summed = lax.psum_scatter(terms, 'tensor', scatter_dimension=1, tiled=True)]
    all_to_all x4 -> x0, waiting for transfers between devices: 9.39 us -> none  [the longest x1 7.15 us: local(): lax.all_to_all(state[2].reshape(nodes, items, drafts, width), 'req', spli...]
    unnamed x42 -> x1, local copies, waits for them, and re-layouts: 6.85 us -> 1.47 us
    reshape x15 -> x0, local copies, waits for them, and re-layouts: 5.12 us -> none  [the longest x1 1.1 us: local(): asked = incoming.reshape(count, heads, HD)]
  transfers between devices with their start and end apart: 6 -> 0, of which waited for: 3 -> 0; matrix products, arithmetic and copies ran while one was open for 38% -> 0% of each run, Pallas kernels for 0% -> 0%
where the time goes in v1:
time: 36.6 us; the launch traced here: 36.5 us
  Pallas kernels  35 us (96%)
  local copies, waits for them, and re-layouts  1.47 us (4%)
    pallas_call x1, Pallas kernels, local(): pl.pallas_call(functools.partial(kernel, n, nt, drafts, cap), out_shape=j...  35 us
    unnamed x1, local copies, waits for them, and re-layouts  1.47 us

profile of v1, /device:TPU:0, one launch (start us, length us, event | category | flops | bytes accessed | tf_op | source)
XLA Modules:
  0.0 36.5 jit_solution(8911384140913186435)
XLA Ops:
  0.0 35.0 %shard_map.118 = bf16[64,512]{1,0:T(8,128)(2,1)} custom-call(bf16[64,1024]{1,0:T(8,128)(2,1)} %tok_ref.1, f32[1,1024]{1,0:T(1,128)} %bitcast.12, bf16[3,1024,512]{2,1,0:T(8,128)(2,1)} %bitcast.9, bf16[512,1024]{1,0:T(8,128)(2,1)} %wout_hbm.1, bf16[64,2,512]{2,1,0:T(2,128)(2,1)} %root_ref.1, bf16[1024,2,512]{2,1,0:T(2,128)(2,1)} %bitcast.10, ...), custom_call_target="tpu_custom_call" | custom-call | tf_op jit(solution)/shard_map/pallas_call | solution.py:461
  35.0 1.5 %copy.14 = bf16[64,512]{1,0:T(8,128)(2,1)} copy(bf16[64,512]{1,0:T(8,128)(2,1)} %shard_map.118) | data formatting | bytes 131072

commit v2 on v1

--- a/solution.py
+++ b/solution.py
@@ -86,8 +86,6 @@
     kroot[me] = own_k
     vroot[me] = own_v
 
-    pl.semaphore_wait(barrier, n - 1 + nt - 1)
-
     core = lax.rem(me, 2)
     chip = lax.div(me, 2)
     zc = lax.div(chip, 2)
@@ -148,12 +146,6 @@
                     send_on(direction, hop + 1, j)
                     offset = -hop if direction == 0 else hop
                     send_share(direction * half + hop, offset, j)
-
-    for j in range(2):
-        for direction in range(2):
-            send_on(direction, 1, j)
-    for j in range(2):
-        send_share(0, 0, j)
 
     floats = tok_ref[...].astype(F32)
     mean = jnp.mean(floats * floats, axis=1, keepdims=True)
@@ -207,10 +199,14 @@
             device_id=(there, tn), device_id_type=MESH,
         )
 
+    pl.semaphore_wait(barrier, n - 1 + nt - 1)
     for j in range(1, n):
         exchange(oq, aq, q_send, q_recv, j, True).start()
-
-    pump(1)
+    for j in range(2):
+        for direction in range(2):
+            send_on(direction, 1, j)
+    for j in range(2):
+        send_share(0, 0, j)
 
     loads[1].wait()
     own_keys = dot(normed, w_ref[1]).astype(BF16)
@@ -230,9 +226,6 @@
         return carry
 
     lax.fori_loop(0, span // piece, part_branch, 0)
-
-    if half >= 2:
-        pump(2)
 
     col_head = lax.div(iota((1, gw), 1), HD)
 
@@ -259,20 +252,63 @@
         sbuf[:amount_of, :length] = dot_t(stacked_rows, keys_of)
 
         def some(c, carry):
-            at = pl.ds(pl.multiple_of(c * step, step), step)
-            s = sbuf[at, :length]
-            if keep is not None:
-                s = jnp.where(keep, s, -1e30)
-            peak = jnp.max(s, axis=1, keepdims=True)
-            w = jnp.exp2((s - peak) * SCALE)
-            peak_buf[at, :] = jnp.broadcast_to(peak, (step, 128))
-            sum_buf[at, :] = jnp.broadcast_to(jnp.sum(w, axis=1, keepdims=True), (step, 128))
-            pbuf[at, :length] = w.astype(BF16)
+            for part in range(0, step, 32):
+                at = pl.ds(pl.multiple_of(c * step + part, 32), 32)
+                s = sbuf[at, :length]
+                if keep is not None:
+                    s = jnp.where(keep, s, -1e30)
+                peak = jnp.max(s, axis=1, keepdims=True)
+                w = jnp.exp2((s - peak) * SCALE)
+                peak_buf[at, :] = jnp.broadcast_to(peak, (32, 128))
+                sum_buf[at, :] = jnp.broadcast_to(jnp.sum(w, axis=1, keepdims=True), (32, 128))
+                pbuf[at, :length] = w.astype(BF16)
             return carry
 
         lax.fori_loop(0, amount_of // step, some, 0)
         weighted = dot(pbuf[:amount_of, :length], values_of)
         return peak_buf[:amount_of, :1], sum_buf[:amount_of, :1], weighted
+
+    loads[4].wait()
+    leaf_rows = requests * leaf_span
+    lpiece = min(128, leaf_rows)
+    lraw_rows = lraw.reshape(2 * leaf_rows, width)
+
+    def part_leaf(b, carry):
+        raw = lraw_rows[pl.ds(pl.multiple_of(2 * lpiece * b, 2 * lpiece), 2 * lpiece), :]
+        k_part, v_part = split_rows(raw, lpiece)
+        at = pl.ds(pl.multiple_of(lpiece * b, lpiece), lpiece)
+        kloc[at, :] = k_part
+        vloc[at, :] = v_part
+        return carry
+
+    lax.fori_loop(0, leaf_rows // lpiece, part_leaf, 0)
+    kloc[pl.ds(leaf_rows, rows), :] = own_keys
+    vloc[pl.ds(leaf_rows, rows), :] = own_values
+    keys = leaf_rows + rows
+    leaf_len = per_row(llen_ref[...])
+    new_count = per_row(newc_ref[...])
+    ki, kj = iota((rows, keys), 0), iota((rows, keys), 1)
+    own_j = kj - leaf_rows
+    draft_j = lax.rem(jnp.maximum(own_j, 0), drafts)
+    in_leaf = (
+        (lax.div(kj, leaf_span) == lax.div(ki, drafts))
+        & (lax.rem(kj, leaf_span).astype(F32) < leaf_len)
+    )
+    in_own = (
+        (lax.div(jnp.maximum(own_j, 0), drafts) == lax.div(ki, drafts))
+        & (draft_j <= lax.rem(ki, drafts))
+        & (draft_j.astype(F32) < new_count)
+    )
+    local_keep = ((kj < leaf_rows) & in_leaf) | ((kj >= leaf_rows) & in_own)
+    stacked = [stack(queries[:, g * gw : (g + 1) * gw].astype(F32)) for g in range(groups)]
+    local_states = []
+    for g in range(groups):
+        cols = slice(g * gw, (g + 1) * gw)
+        scores = dot_t(stacked[g], kloc[:, cols])
+        pieces = [scores[h * rows : (h + 1) * rows] for h in range(hg)]
+        local_states.append(attend(pieces, [local_keep] * hg, vloc[:, cols]))
+
+    pump(1)
 
     for j in range(1, n):
         exchange(oq, aq, q_send, q_recv, j, False).wait_recv()
@@ -302,8 +338,8 @@
         stats = jnp.where(lane < hg, high, jnp.where(lane < 2 * hg, middle, low))
         stats = jnp.where(lane < 3 * hg, stats, 0.0)
         slabs.append(jnp.concatenate([mixed, stats], axis=1).reshape(n, cd, gw + 128))
-        if half >= 3 and g == 0:
-            pump(3)
+        if half >= 2 and g == 0:
+            pump(2)
     if groups * cd < slot:
         slabs.append(jnp.zeros((n, slot - groups * cd, gw + 128), F32))
     bo[...] = jnp.concatenate(slabs, axis=1).astype(BF16)
@@ -311,49 +347,8 @@
     for j in range(1, n):
         exchange(bo, br, b_send, b_recv, j, True).start()
 
-    loads[4].wait()
-    leaf_rows = requests * leaf_span
-    lpiece = min(128, leaf_rows)
-    lraw_rows = lraw.reshape(2 * leaf_rows, width)
-
-    def part_leaf(b, carry):
-        raw = lraw_rows[pl.ds(pl.multiple_of(2 * lpiece * b, 2 * lpiece), 2 * lpiece), :]
-        k_part, v_part = split_rows(raw, lpiece)
-        at = pl.ds(pl.multiple_of(lpiece * b, lpiece), lpiece)
-        kloc[at, :] = k_part
-        vloc[at, :] = v_part
-        return carry
-
-    lax.fori_loop(0, leaf_rows // lpiece, part_leaf, 0)
-    kloc[pl.ds(leaf_rows, rows), :] = own_keys
-    vloc[pl.ds(leaf_rows, rows), :] = own_values
-    keys = leaf_rows + rows
-    leaf_len = per_row(llen_ref[...])
-    new_count = per_row(newc_ref[...])
-    ki, kj = iota((rows, keys), 0), iota((rows, keys), 1)
-    own_j = kj - leaf_rows
-    draft_j = lax.rem(jnp.maximum(own_j, 0), drafts)
-    in_leaf = (
-        (lax.div(kj, leaf_span) == lax.div(ki, drafts))
-        & (lax.rem(kj, leaf_span).astype(F32) < leaf_len)
-    )
-    in_own = (
-        (lax.div(jnp.maximum(own_j, 0), drafts) == lax.div(ki, drafts))
-        & (draft_j <= lax.rem(ki, drafts))
-        & (draft_j.astype(F32) < new_count)
-    )
-    local_keep = ((kj < leaf_rows) & in_leaf) | ((kj >= leaf_rows) & in_own)
-    stacked = [stack(queries[:, g * gw : (g + 1) * gw].astype(F32)) for g in range(groups)]
-    local_states = []
-    for g in range(groups):
-        cols = slice(g * gw, (g + 1) * gw)
-        scores = dot_t(stacked[g], kloc[:, cols])
-        pieces = [scores[h * rows : (h + 1) * rows] for h in range(hg)]
-        local_states.append(attend(pieces, [local_keep] * hg, vloc[:, cols]))
-
-    for hop in range(1 if half < 2 else 4 if half >= 3 else 3, half + 1):
-        if hop > 1:
-            pump(hop)
+    for hop in range(3, half + 1):
+        pump(hop)
     for index, offset, j in shared:
         share(index, offset, j, False).wait_recv()
 
@@ -362,7 +357,7 @@
         cols = slice(g * gw, (g + 1) * gw)
         root_keys = kroot[:, :, cols].reshape(n * block, gw)
         root_values = vroot[:, :, cols].reshape(n * block, gw)
-        peaks, sums, weighted = attend_long(stacked[g], root_keys, root_values, None, rows)
+        peaks, sums, weighted = attend_long(stacked[g], root_keys, root_values, None, min(128, hg * rows))
         lpeaks, lsums, lweighted = local_states[g]
         level = jnp.zeros((rows, gw), F32)
         amount = jnp.zeros((rows, gw), F32)
@@ -406,8 +401,6 @@
         heads.append(((one * mixed + two * got[:, :gw]) / (one * amount + two)).astype(BF16))
     attention = heads[0] if groups == 1 else jnp.concatenate(heads, axis=1)
     ow = out_ref.shape[1]
-    for t in range(nt):
-        tb[t] = dot(attention, wout_ref[:, t * ow : (t + 1) * ow])
 
     def reduce_copy(j, outgoing):
         there = lax.rem(tn + j, nt)
@@ -418,10 +411,15 @@
             device_id=(me, there), device_id_type=MESH,
         )
 
+    def term(t):
+        return dot(attention, wout_ref[:, pl.ds(pl.multiple_of(t * ow, ow), ow)])
+
     for j in range(1, nt):
+        there = lax.rem(tn + j, nt)
+        tb[there] = term(there).astype(BF16)
         reduce_copy(j, True).start()
     in_use = lax.rem(iota((rows, 1), 0), drafts).astype(F32) < new_count
-    result = tb[tn]
+    result = term(tn)
     for copy in sent:
         copy.wait_send()
     for j in range(1, n):
@@ -429,7 +427,7 @@
         exchange(bo, br, b_send, b_recv, j, True).wait_send()
     for j in range(1, nt):
         reduce_copy(j, False).wait_recv()
-        result = result + tr[lax.rem(tn + nt - j, nt)]
+        result = result + tr[lax.rem(tn + nt - j, nt)].astype(F32)
     out_ref[...] = jnp.where(in_use, result, 0.0).astype(BF16)
     for j in range(1, nt):
         reduce_copy(j, True).wait_send()
@@ -478,8 +476,8 @@
             pltpu.VMEM((n, slot, gw), BF16),
             pltpu.VMEM((n, slot, gw + 128), BF16),
             pltpu.VMEM((n, slot, gw + 128), BF16),
-            pltpu.VMEM((nt, rows, ow), F32),
-            pltpu.VMEM((nt, rows, ow), F32),
+            pltpu.VMEM((nt, rows, ow), BF16),
+            pltpu.VMEM((nt, rows, ow), BF16),
             pltpu.VMEM((long_rows, longest), F32),
             pltpu.VMEM((long_rows, longest), BF16),
             pltpu.VMEM((long_rows, 128), F32),

time: 36.6 us -> 37.4 us (1.022)
  Pallas kernels: 35 us -> 35.8 us
    pallas_call x1, Pallas kernels: 35 us -> 35.8 us  [local(): pl.pallas_call(functools.partial(kernel, n, nt, drafts, cap), out_shape=j...]
where the time goes in v2:
time: 37.4 us; the launch traced here: 37.3 us
  Pallas kernels  35.8 us (96%)
  local copies, waits for them, and re-layouts  1.47 us (4%)
    pallas_call x1, Pallas kernels, local(): pl.pallas_call(functools.partial(kernel, n, nt, drafts, cap), out_shape=j...  35.8 us
    unnamed x1, local copies, waits for them, and re-layouts  1.47 us

profile of v2, /device:TPU:0, one launch (start us, length us, event | category | flops | bytes accessed | tf_op | source)
XLA Modules:
  0.0 37.3 jit_solution(10794107096611702352)
XLA Ops:
  0.0 35.8 %shard_map.118 = bf16[64,512]{1,0:T(8,128)(2,1)} custom-call(bf16[64,1024]{1,0:T(8,128)(2,1)} %tok_ref.1, f32[1,1024]{1,0:T(1,128)} %bitcast.12, bf16[3,1024,512]{2,1,0:T(8,128)(2,1)} %bitcast.9, bf16[512,1024]{1,0:T(8,128)(2,1)} %wout_hbm.1, bf16[64,2,512]{2,1,0:T(2,128)(2,1)} %root_ref.1, bf16[1024,2,512]{2,1,0:T(2,128)(2,1)} %bitcast.10, ...), custom_call_target="tpu_custom_call" | custom-call | tf_op jit(solution)/shard_map/pallas_call | solution.py:459
  35.8 1.5 %copy.14 = bf16[64,512]{1,0:T(8,128)(2,1)} copy(bf16[64,512]{1,0:T(8,128)(2,1)} %shard_map.118) | data formatting | bytes 131072

commit v3 on v2

--- a/solution.py
+++ b/solution.py
@@ -20,6 +20,14 @@
     return lax.broadcasted_iota(jnp.int32, shape, dim)
 
 
+def div(a, by):
+    return a >> (by.bit_length() - 1) if by & (by - 1) == 0 else lax.div(a, by)
+
+
+def rem(a, by):
+    return a & (by - 1) if by & (by - 1) == 0 else lax.rem(a, by)
+
+
 def dot(a, b):
     return jnp.dot(a, b, preferred_element_type=F32)
 
@@ -33,9 +41,9 @@
     tok_ref, gain_ref, w_hbm, wout_hbm, root_ref, bkv_hbm, leaf_hbm,
     branch_ref, owner_ref, blen_ref, llen_ref, newc_ref,
     out_ref,
-    w_ref, wout_ref, braw, lraw, kroot, vroot, kbr, vbr, kloc, vloc,
+    w_ref, wout_ref, braw, lraw, kvroot, kbr, vbr, kloc, vloc,
     oq, aq, bo, br, tb, tr, sbuf, pbuf, peak_buf, sum_buf, asked,
-    local_sem, ring_send, ring_recv, sib_send, sib_recv,
+    local_sem, root_send, ring_recv, sib_recv,
     q_send, q_recv, b_send, b_recv, t_send, t_recv,
 ):
     rows = tok_ref.shape[0]
@@ -75,16 +83,20 @@
             barrier, inc=1, device_id=(me, lax.rem(tn + j, nt)), device_id_type=MESH
         )
 
-    def split_rows(raw, count):
+    def splitter(count):
         pick = iota((2 * count, 2 * count), 0)
         col = iota((2 * count, 2 * count), 1)
         source = jnp.where(pick < count, 2 * pick, 2 * (pick - count) + 1)
-        parted = dot((col == source).astype(BF16), raw).astype(BF16)
+        return (col == source).astype(BF16)
+
+    def split_rows(chosen, raw):
+        count = raw.shape[0] // 2
+        parted = dot(chosen, raw).astype(BF16)
         return parted[:count], parted[count:]
 
-    own_k, own_v = split_rows(root_ref.reshape(2 * block, width)[...], block)
-    kroot[me] = own_k
-    vroot[me] = own_v
+    own_k, own_v = split_rows(splitter(block), root_ref.reshape(2 * block, width)[...])
+    kvroot[me, 0] = own_k
+    kvroot[me, 1] = own_v
 
     core = lax.rem(me, 2)
     chip = lax.div(me, 2)
@@ -99,53 +111,44 @@
         return (zq * 2 + xq) * 2 + core
 
     sibling = me + 1 - 2 * core
-    stores = (kroot, vroot)
-
-    def ring(direction, hop, j, outgoing):
+
+    def ring(direction, hop, outgoing):
         sign = 1 - 2 * direction
         origin = device_at(place - sign * (hop - 1 if outgoing else hop))
+        part = kvroot.at[origin] if hop < half else kvroot.at[origin, direction]
         return pltpu.make_async_remote_copy(
-            src_ref=stores[j].at[origin], dst_ref=stores[j].at[origin],
-            send_sem=ring_send.at[direction, hop, j], recv_sem=ring_recv.at[direction, hop, j],
+            src_ref=part, dst_ref=part,
+            send_sem=root_send.at[0], recv_sem=ring_recv.at[direction, hop],
             device_id=(device_at(place + sign), tn), device_id_type=MESH,
         )
 
-    def share(index, offset, j, outgoing):
+    def share(index, offset, outgoing):
         origin = device_at(place + offset)
         if not outgoing:
             origin = origin + 1 - 2 * core
         return pltpu.make_async_remote_copy(
-            src_ref=stores[j].at[origin], dst_ref=stores[j].at[origin],
-            send_sem=sib_send.at[index, j], recv_sem=sib_recv.at[index, j],
+            src_ref=kvroot.at[origin], dst_ref=kvroot.at[origin],
+            send_sem=root_send.at[0], recv_sem=sib_recv.at[index],
             device_id=(sibling, tn), device_id_type=MESH,
         )
 
-    def travels(direction, hop, j):
-        return hop < half or (hop == half and j == direction)
-
-    sent = []
-    shared = []
-
-    def send_on(direction, hop, j):
-        if travels(direction, hop, j):
-            copy = ring(direction, hop, j, True)
-            copy.start()
-            sent.append(copy)
-
-    def send_share(index, offset, j):
-        copy = share(index, offset, j, True)
-        copy.start()
-        sent.append(copy)
-        shared.append((index, offset, j))
+    shared = [(0, 0)]
+    shared += [(k, -k) for k in range(1, half + 1)]
+    shared += [(half + k, k) for k in range(1, half)]
 
     def pump(hop):
-        for j in range(2):
-            for direction in range(2):
-                if travels(direction, hop, j):
-                    ring(direction, hop, j, False).wait_recv()
-                    send_on(direction, hop + 1, j)
-                    offset = -hop if direction == 0 else hop
-                    send_share(direction * half + hop, offset, j)
+        for direction in range(2):
+            ring(direction, hop, False).wait_recv()
+            if hop < half:
+                ring(direction, hop + 1, True).start()
+                share(direction * half + hop, hop * (2 * direction - 1), True).start()
+        if hop == half:
+            share(half, -half, True).start()
+
+    pl.semaphore_wait(barrier, n - 1 + nt - 1)
+    for direction in range(2):
+        ring(direction, 1, True).start()
+    share(0, 0, True).start()
 
     floats = tok_ref[...].astype(F32)
     mean = jnp.mean(floats * floats, axis=1, keepdims=True)
@@ -153,7 +156,7 @@
     loads[0].wait()
     queries = dot(normed, w_ref[0]).astype(BF16)
 
-    row_req = lax.div(iota((rows, requests), 0), drafts)
+    row_req = div(iota((rows, requests), 0), drafts)
     at_req = row_req == iota((rows, requests), 1)
 
     def per_row(values):
@@ -166,22 +169,22 @@
     target_t = dot_t(owners, chosen).astype(BF16)
     same = dot_t(target, target)
     ri, rj = iota((rows, rows), 0), iota((rows, rows), 1)
-    qi, qj = lax.div(ri, drafts), lax.div(rj, drafts)
-    first_j = lax.rem(rj, drafts) == 0
-    first_i = lax.rem(ri, drafts) == 0
+    qi, qj = div(ri, drafts), div(rj, drafts)
+    first_j = rem(rj, drafts) == 0
+    first_i = rem(ri, drafts) == 0
     order_col = jnp.sum(jnp.where((qj < qi) & first_j, same, 0.0), axis=1, keepdims=True)
     order_row = jnp.sum(jnp.where((qi < qj) & first_i, same, 0.0), axis=0, keepdims=True)
     total = n * slot
-    spread = (lax.div(iota((total, n), 0), slot) == iota((total, n), 1)).astype(BF16)
+    spread = (div(iota((total, n), 0), slot) == iota((total, n), 1)).astype(BF16)
 
     def slot_parts(shape, dim):
-        inner = lax.rem(iota(shape, dim), slot)
-        item = lax.rem(inner, cd)
-        return lax.div(inner, cd), lax.div(item, drafts).astype(F32), lax.rem(item, drafts)
+        inner = rem(iota(shape, dim), slot)
+        item = rem(inner, cd)
+        return div(inner, cd), div(item, drafts).astype(F32), rem(item, drafts)
 
     group_k, item_k, draft_k = slot_parts((total, rows), 0)
     put = (dot(spread, target_t) > 0.5) & (order_row == item_k) & (
-        lax.rem(iota((total, rows), 1), drafts) == draft_k
+        rem(iota((total, rows), 1), drafts) == draft_k
     )
     packed = jnp.zeros((total, gw), F32)
     for g in range(groups):
@@ -190,23 +193,24 @@
     oq[...] = packed.astype(BF16).reshape(n, slot, gw)
     aq[me] = oq[me]
 
-    def exchange(source, landing, send_sem, recv_sem, j, outgoing):
+    def exchange(source, landing, send_sem, recv_sem, j):
         there = lax.rem(me + j, n)
-        here = me if outgoing else lax.rem(me + n - j, n)
         return pltpu.make_async_remote_copy(
-            src_ref=source.at[there], dst_ref=landing.at[here],
-            send_sem=send_sem.at[j], recv_sem=recv_sem.at[j],
+            src_ref=source.at[there], dst_ref=landing.at[me],
+            send_sem=send_sem.at[0], recv_sem=recv_sem.at[0],
             device_id=(there, tn), device_id_type=MESH,
         )
 
-    pl.semaphore_wait(barrier, n - 1 + nt - 1)
+    def of_all(source, landing, send_sem, recv_sem):
+        return pltpu.make_async_remote_copy(
+            src_ref=source.at[pl.ds(0, n - 1)], dst_ref=landing.at[pl.ds(0, n - 1)],
+            send_sem=send_sem.at[0], recv_sem=recv_sem.at[0],
+            device_id=(lax.rem(me + 1, n), tn), device_id_type=MESH,
+        )
+
     for j in range(1, n):
-        exchange(oq, aq, q_send, q_recv, j, True).start()
-    for j in range(2):
-        for direction in range(2):
-            send_on(direction, 1, j)
-    for j in range(2):
-        send_share(0, 0, j)
+        exchange(oq, aq, q_send, q_recv, j).start()
+    pump(1)
 
     loads[1].wait()
     own_keys = dot(normed, w_ref[1]).astype(BF16)
@@ -217,9 +221,11 @@
     piece = min(128, span)
     braw_rows = braw.reshape(2 * span, width)
 
+    branch_pick = splitter(piece)
+
     def part_branch(b, carry):
         raw = braw_rows[pl.ds(pl.multiple_of(2 * piece * b, 2 * piece), 2 * piece), :]
-        k_part, v_part = split_rows(raw, piece)
+        k_part, v_part = split_rows(branch_pick, raw)
         at = pl.ds(pl.multiple_of(piece * b, piece), piece)
         kbr[at, :] = k_part
         vbr[at, :] = v_part
@@ -227,7 +233,7 @@
 
     lax.fori_loop(0, span // piece, part_branch, 0)
 
-    col_head = lax.div(iota((1, gw), 1), HD)
+    col_head = div(iota((1, gw), 1), HD)
 
     def stack(part):
         return jnp.concatenate(
@@ -273,9 +279,11 @@
     lpiece = min(128, leaf_rows)
     lraw_rows = lraw.reshape(2 * leaf_rows, width)
 
+    leaf_pick = branch_pick if lpiece == piece else splitter(lpiece)
+
     def part_leaf(b, carry):
         raw = lraw_rows[pl.ds(pl.multiple_of(2 * lpiece * b, 2 * lpiece), 2 * lpiece), :]
-        k_part, v_part = split_rows(raw, lpiece)
+        k_part, v_part = split_rows(leaf_pick, raw)
         at = pl.ds(pl.multiple_of(lpiece * b, lpiece), lpiece)
         kloc[at, :] = k_part
         vloc[at, :] = v_part
@@ -289,14 +297,14 @@
     new_count = per_row(newc_ref[...])
     ki, kj = iota((rows, keys), 0), iota((rows, keys), 1)
     own_j = kj - leaf_rows
-    draft_j = lax.rem(jnp.maximum(own_j, 0), drafts)
+    draft_j = rem(jnp.maximum(own_j, 0), drafts)
     in_leaf = (
-        (lax.div(kj, leaf_span) == lax.div(ki, drafts))
-        & (lax.rem(kj, leaf_span).astype(F32) < leaf_len)
+        (div(kj, leaf_span) == div(ki, drafts))
+        & (rem(kj, leaf_span).astype(F32) < leaf_len)
     )
     in_own = (
-        (lax.div(jnp.maximum(own_j, 0), drafts) == lax.div(ki, drafts))
-        & (draft_j <= lax.rem(ki, drafts))
+        (div(jnp.maximum(own_j, 0), drafts) == div(ki, drafts))
+        & (draft_j <= rem(ki, drafts))
         & (draft_j.astype(F32) < new_count)
     )
     local_keep = ((kj < leaf_rows) & in_leaf) | ((kj >= leaf_rows) & in_own)
@@ -308,10 +316,10 @@
         pieces = [scores[h * rows : (h + 1) * rows] for h in range(hg)]
         local_states.append(attend(pieces, [local_keep] * hg, vloc[:, cols]))
 
-    pump(1)
-
-    for j in range(1, n):
-        exchange(oq, aq, q_send, q_recv, j, False).wait_recv()
+    if half >= 2:
+        pump(2)
+
+    of_all(oq, aq, q_send, q_recv).wait_recv()
     asked[...] = aq[...].astype(F32)
     owned = jnp.sum(
         jnp.where(owner_ref[...] == me, blen_ref[...], 0).astype(F32), axis=1, keepdims=True
@@ -331,32 +339,32 @@
         for h in range(hg):
             at = slice(h * count, (h + 1) * count)
             mixed = jnp.where(col_head == h, weighted[at] * inverse[at], mixed)
-            levels = jnp.where(lax.rem(lane, hg) == h, level[at], levels)
+            levels = jnp.where(rem(lane, hg) == h, level[at], levels)
         high = levels.astype(BF16).astype(F32)
         middle = (levels - high).astype(BF16).astype(F32)
         low = levels - high - middle
         stats = jnp.where(lane < hg, high, jnp.where(lane < 2 * hg, middle, low))
         stats = jnp.where(lane < 3 * hg, stats, 0.0)
         slabs.append(jnp.concatenate([mixed, stats], axis=1).reshape(n, cd, gw + 128))
-        if half >= 2 and g == 0:
-            pump(2)
+        if half >= 3 and g == 0:
+            pump(3)
     if groups * cd < slot:
         slabs.append(jnp.zeros((n, slot - groups * cd, gw + 128), F32))
     bo[...] = jnp.concatenate(slabs, axis=1).astype(BF16)
     br[me] = bo[me]
     for j in range(1, n):
-        exchange(bo, br, b_send, b_recv, j, True).start()
-
-    for hop in range(3, half + 1):
+        exchange(bo, br, b_send, b_recv, j).start()
+
+    for hop in range(4, half + 1):
         pump(hop)
-    for index, offset, j in shared:
-        share(index, offset, j, False).wait_recv()
+    for index, offset in shared:
+        share(index, offset, False).wait_recv()
 
     before = []
     for g in range(groups):
         cols = slice(g * gw, (g + 1) * gw)
-        root_keys = kroot[:, :, cols].reshape(n * block, gw)
-        root_values = vroot[:, :, cols].reshape(n * block, gw)
+        root_keys = kvroot[:, 0, :, cols].reshape(n * block, gw)
+        root_values = kvroot[:, 1, :, cols].reshape(n * block, gw)
         peaks, sums, weighted = attend_long(stacked[g], root_keys, root_values, None, min(128, hg * rows))
         lpeaks, lsums, lweighted = local_states[g]
         level = jnp.zeros((rows, gw), F32)
@@ -374,13 +382,12 @@
 
     group_l, item_l, draft_l = slot_parts((rows, total), 1)
     take = (dot_t(target, spread) > 0.5) & (order_col == item_l) & (
-        lax.rem(iota((rows, total), 0), drafts) == draft_l
+        rem(iota((rows, total), 0), drafts) == draft_l
     )
     takes = [jnp.where(take & (group_l == g), 1.0, 0.0).astype(BF16) for g in range(groups)]
     loads[5].wait()
 
-    for j in range(1, n):
-        exchange(bo, br, b_send, b_recv, j, False).wait_recv()
+    of_all(bo, br, b_send, b_recv).wait_recv()
     flat = br[...].reshape(total, gw + 128)
     heads = []
     for g in range(groups):
@@ -418,13 +425,11 @@
         there = lax.rem(tn + j, nt)
         tb[there] = term(there).astype(BF16)
         reduce_copy(j, True).start()
-    in_use = lax.rem(iota((rows, 1), 0), drafts).astype(F32) < new_count
+    in_use = rem(iota((rows, 1), 0), drafts).astype(F32) < new_count
     result = term(tn)
-    for copy in sent:
-        copy.wait_send()
-    for j in range(1, n):
-        exchange(oq, aq, q_send, q_recv, j, True).wait_send()
-        exchange(bo, br, b_send, b_recv, j, True).wait_send()
+    of_all(kvroot, kvroot, root_send, root_send).wait_send()
+    of_all(oq, aq, q_send, q_recv).wait_send()
+    of_all(bo, br, b_send, b_recv).wait_send()
     for j in range(1, nt):
         reduce_copy(j, False).wait_recv()
         result = result + tr[lax.rem(tn + nt - j, nt)].astype(F32)
@@ -466,8 +471,7 @@
             pltpu.VMEM(w_out.shape, BF16),
             pltpu.VMEM((span, 2, width), BF16),
             pltpu.VMEM((leaf_rows, 2, width), BF16),
-            pltpu.VMEM((n, block, width), BF16),
-            pltpu.VMEM((n, block, width), BF16),
+            pltpu.VMEM((n, 2, block, width), BF16),
             pltpu.VMEM((span, width), BF16),
             pltpu.VMEM((span, width), BF16),
             pltpu.VMEM((leaf_rows + rows, width), BF16),
@@ -484,14 +488,13 @@
             pltpu.VMEM((long_rows, 128), F32),
             pltpu.VMEM((n, slot, gw), F32),
             dma((6,)),
-            dma((2, half + 1, 2)),
-            dma((2, half + 1, 2)),
-            dma((2 * half + 1, 2)),
-            dma((2 * half + 1, 2)),
-            dma((n,)),
-            dma((n,)),
-            dma((n,)),
-            dma((n,)),
+            dma((1,)),
+            dma((2, half + 1)),
+            dma((2 * half,)),
+            dma((1,)),
+            dma((1,)),
+            dma((1,)),
+            dma((1,)),
             dma((nt,)),
             dma((nt,)),
         ],

time: 37.4 us -> 35 us (0.936)
  Pallas kernels: 35.8 us -> 33.4 us
    pallas_call x1, Pallas kernels: 35.8 us -> 33.4 us  [local(): pl.pallas_call(functools.partial(kernel, n, nt, drafts, cap), out_shape=j...]
where the time goes in v3:
time: 35 us; the launch traced here: 34.9 us
  Pallas kernels  33.4 us (95%)
  local copies, waits for them, and re-layouts  1.47 us (4%)
    pallas_call x1, Pallas kernels, local(): pl.pallas_call(functools.partial(kernel, n, nt, drafts, cap), out_shape=j...  33.4 us
    unnamed x1, local copies, waits for them, and re-layouts  1.47 us

profile of v3, /device:TPU:0, one launch (start us, length us, event | category | flops | bytes accessed | tf_op | source)
XLA Modules:
  0.0 34.9 jit_solution(13299504087331580417)
XLA Ops:
  0.0 33.4 %shard_map.118 = bf16[64,512]{1,0:T(8,128)(2,1)} custom-call(bf16[64,1024]{1,0:T(8,128)(2,1)} %tok_ref.1, f32[1,1024]{1,0:T(1,128)} %bitcast.12, bf16[3,1024,512]{2,1,0:T(8,128)(2,1)} %bitcast.9, bf16[512,1024]{1,0:T(8,128)(2,1)} %wout_hbm.1, bf16[64,2,512]{2,1,0:T(2,128)(2,1)} %root_ref.1, bf16[1024,2,512]{2,1,0:T(2,128)(2,1)} %bitcast.10, ...), custom_call_target="tpu_custom_call" | custom-call | tf_op jit(solution)/shard_map/pallas_call | solution.py:464
  33.4 1.5 %copy.14 = bf16[64,512]{1,0:T(8,128)(2,1)} copy(bf16[64,512]{1,0:T(8,128)(2,1)} %shard_map.118) | data formatting | bytes 131072

commit v4 on v3

--- a/solution.py
+++ b/solution.py
@@ -66,7 +66,7 @@
     loads.append(pltpu.make_async_copy(bkv_hbm, braw, local_sem.at[3]))
     loads.append(pltpu.make_async_copy(leaf_hbm, lraw, local_sem.at[4]))
     loads.append(pltpu.make_async_copy(wout_hbm, wout_ref, local_sem.at[5]))
-    for load in loads:
+    for load in loads[:3]:
         load.start()
 
     barrier = pltpu.get_barrier_semaphore()
@@ -154,6 +154,8 @@
     mean = jnp.mean(floats * floats, axis=1, keepdims=True)
     normed = (floats * lax.rsqrt(mean + 1e-05) * gain_ref[...]).astype(BF16)
     loads[0].wait()
+    for load in loads[3:]:
+        load.start()
     queries = dot(normed, w_ref[0]).astype(BF16)
 
     row_req = div(iota((rows, requests), 0), drafts)
@@ -231,7 +233,7 @@
         vbr[at, :] = v_part
         return carry
 
-    lax.fori_loop(0, span // piece, part_branch, 0)
+    lax.fori_loop(0, span // piece, part_branch, 0, unroll=2)
 
     col_head = div(iota((1, gw), 1), HD)
 
@@ -289,7 +291,7 @@
         vloc[at, :] = v_part
         return carry
 
-    lax.fori_loop(0, leaf_rows // lpiece, part_leaf, 0)
+    lax.fori_loop(0, leaf_rows // lpiece, part_leaf, 0, unroll=2)
     kloc[pl.ds(leaf_rows, rows), :] = own_keys
     vloc[pl.ds(leaf_rows, rows), :] = own_values
     keys = leaf_rows + rows
@@ -331,7 +333,7 @@
     for g in range(groups):
         part = asked[:, g * cd : (g + 1) * cd, :].reshape(count, gw)
         cols = slice(g * gw, (g + 1) * gw)
-        peaks, sums, weighted = attend_long(stack(part), kbr[:, cols], vbr[:, cols], usable, 128)
+        peaks, sums, weighted = attend_long(stack(part), kbr[:, cols], vbr[:, cols], usable, 256)
         inverse = 1.0 / sums
         level = peaks * SCALE + jnp.log(sums) * LOG2E
         mixed = jnp.zeros((count, gw), F32)
@@ -365,7 +367,7 @@
         cols = slice(g * gw, (g + 1) * gw)
         root_keys = kvroot[:, 0, :, cols].reshape(n * block, gw)
         root_values = kvroot[:, 1, :, cols].reshape(n * block, gw)
-        peaks, sums, weighted = attend_long(stacked[g], root_keys, root_values, None, min(128, hg * rows))
+        peaks, sums, weighted = attend_long(stacked[g], root_keys, root_values, None, min(256, hg * rows))
         lpeaks, lsums, lweighted = local_states[g]
         level = jnp.zeros((rows, gw), F32)
         amount = jnp.zeros((rows, gw), F32)

time: 35 us -> 35.5 us (1.014)
  Pallas kernels: 33.4 us -> 33.8 us
    pallas_call x1, Pallas kernels: 33.4 us -> 33.8 us  [local(): pl.pallas_call(functools.partial(kernel, n, nt, drafts, cap), out_shape=j...]
where the time goes in v4:
time: 35.5 us; the launch traced here: 35.3 us
  Pallas kernels  33.8 us (95%)
  local copies, waits for them, and re-layouts  1.47 us (4%)
    pallas_call x1, Pallas kernels, local(): pl.pallas_call(functools.partial(kernel, n, nt, drafts, cap), out_shape=j...  33.8 us
    unnamed x1, local copies, waits for them, and re-layouts  1.47 us

profile of v4, /device:TPU:0, one launch (start us, length us, event | category | flops | bytes accessed | tf_op | source)
XLA Modules:
  0.0 35.3 jit_solution(2387819710482742947)
XLA Ops:
  0.0 33.8 %shard_map.118 = bf16[64,512]{1,0:T(8,128)(2,1)} custom-call(bf16[64,1024]{1,0:T(8,128)(2,1)} %tok_ref.1, f32[1,1024]{1,0:T(1,128)} %bitcast.12, bf16[3,1024,512]{2,1,0:T(8,128)(2,1)} %bitcast.9, bf16[512,1024]{1,0:T(8,128)(2,1)} %wout_hbm.1, bf16[64,2,512]{2,1,0:T(2,128)(2,1)} %root_ref.1, bf16[1024,2,512]{2,1,0:T(2,128)(2,1)} %bitcast.10, ...), custom_call_target="tpu_custom_call" | custom-call | tf_op jit(solution)/shard_map/pallas_call | solution.py:466
  33.8 1.5 %copy.14 = bf16[64,512]{1,0:T(8,128)(2,1)} copy(bf16[64,512]{1,0:T(8,128)(2,1)} %shard_map.118) | data formatting | bytes 131072
